TPU v7x, 256 devices: a whole 4x4x8 slice. The times are simulated.
256 devices in a mesh: mic: 16 (over z, x_hi), tm: 16 (over y, x_lo, core).
Axes of the slice: x: 4 (x_hi: 2, x_lo: 2; x = x_hi * 2 + x_lo), y: 4, z: 8, core: 2. Of those that a mesh axis runs over, the one named last changes fastest.
Arguments:
- signal: bfloat16 [512, 32768], P('mic', 'tm'), may hold values from -6 to 6
- delay: int32 [128, 512, 1024], P('tm', 'mic'), may hold values from 0 to 56
- fraction: float32 [512, 1024], P('mic'), may hold values from 0 to 1
- weight: float32 [512, 1024], P('mic'), may hold values from -0.25 to 0.25
Outputs:
- beam: float32 [1024, 32768], P('mic', 'tm')
Inputs may be any that keep to these rules, and one draw needn't show every extreme that they name: Each delay leaves room for the eight taps inside the span of 64 samples.
All inputs are finite; a program needn't handle non-finite values.
Results may differ from a plain program's by a relative error of at most 0.0029.
Values may be sent and summed in bfloat16 or wider, within the bound.
A program may use at most 320 MiB of HBM per device.

v0:
```python
import math

import jax
import jax.numpy as jnp
from jax import lax
from jax.experimental import pallas as pl
from jax.experimental.pallas import tpu as pltpu
from jax.sharding import PartitionSpec as P

MESH = pl.DeviceIdType.MESH
BF, F32, I16 = jnp.bfloat16, jnp.float32, jnp.int16
MICS, FOCUS, HALF, NB, SUB, TIME = 32, 1024, 512, 8, 256, 2048
RING = 8
WIDE = TIME + 128


def series(y, terms):
    r = jnp.full_like(y, terms[-1])
    for c in terms[-2::-1]:
        r = r * y + c
    return r


SIN = [(-1) ** k * math.pi ** (2 * k + 1) / math.factorial(2 * k + 1) for k in range(7)]
COS = [(-1) ** k * math.pi ** (2 * k) / math.factorial(2 * k) for k in range(6)]


def eight_taps(frac, weight):
    low = jnp.minimum(frac, 1.0 - frac)
    scaled = series(low * low, SIN) * low * weight * (1.0 / math.pi)
    quarter = frac * 0.25
    square = quarter * quarter
    s, c = series(square, SIN) * quarter, series(square, COS)
    taps = []
    for r in range(8):
        x = (r - 3.0) - frac
        a = math.pi * (r - 3) / 4.0
        window = 0.5 + (0.5 * math.cos(a)) * c + (0.5 * math.sin(a)) * s
        tap = (scaled if r % 2 == 0 else -scaled) / x * window
        if r in (3, 4):
            tap = jnp.where(x == 0.0, weight, tap)
        taps.append(tap.astype(BF))
    return taps


def tile(mh, fc):
    return pl.ds(mh * 16, 16), pl.ds(fc * 128, 128)


def fill_taps(fw, taps):
    for mh in range(2):
        for fc in range(4):
            rows, cols = tile(mh, fc)
            for p, t in enumerate(eight_taps(fw[0, rows, cols], fw[1, rows, cols])):
                taps[p, rows, cols] = t


def coefficients(taps, delay):
    zero = jnp.zeros((16, 128), BF)
    columns = []
    for fc in range(4):
        parts = []
        for mh in range(2):
            rows, cols = tile(mh, fc)
            t = [taps[p, rows, cols] for p in range(8)]
            d = delay[rows, cols]
            at = [(d + I16(7 - q)) >> I16(3) for q in range(8)]
            for bit in (4, 2, 1):
                on = (d & I16(bit)) != I16(0)
                t = [jnp.where(on, t[(q - bit) % 8], t[q]) for q in range(8)]
            parts.append((t, at))
        columns.append(
            jnp.concatenate(
                [jnp.where(at[q] == I16(h), t[q], zero) for h in range(8) for q in range(8) for t, at in parts],
                axis=0,
            )
        )
    return jnp.concatenate(columns, axis=1)


def spread(sig, b, g, hh):
    s = sig[:, pl.ds(pl.multiple_of(b * SUB, 128), 384)].astype(F32)
    g[...] = jnp.concatenate([s] + [pltpu.roll(s, 384 - k, 1) for k in range(1, 4)], axis=0).T
    for k in range(4):
        hh[:, pl.ds(k * 128, 128)] = g[pl.ds(4 * k, 304), :].astype(BF)


def block_dot(hh, taps, delay):
    lhs = jnp.concatenate([hh[pl.ds(16 * k, SUB), :] for k in range(4)], axis=1)
    return jnp.dot(lhs, coefficients(taps, delay), preferred_element_type=F32)


def halves(wide, put):
    lane = lax.broadcasted_iota(jnp.int32, (MICS, 128), 1)
    for i in range(4):
        c0, c1 = wide(2 * i), wide(2 * i + 1)
        put(0, i, jnp.where(lane < 64, c0, pltpu.roll(c1, 64, 1)))
        put(1, i, jnp.where(lane < 64, pltpu.roll(c0, 64, 1), c1))


def kernel(signal, delay, fraction, weight, out,
           sig, psig, raw, dly, pdly, fwraw, fw, pfw, taps, ptaps, g, hh, own, part, sbuf, rbuf,
           lsem, xs, xr, ds_, dr, gs, gr, hs, hr, ss, rs):
    mic, tm = lax.axis_index("mic"), lax.axis_index("tm")
    z, h = mic // 2, lax.rem(mic, 2)
    other = z * 2 + 1 - h
    right = lax.rem(z + 1, RING) * 2 + h
    left = lax.rem(z + RING - 1, RING) * 2 + h
    ntm = lax.axis_size("tm")

    bar = pltpu.get_barrier_semaphore()
    for peer in (other, right, left):
        pl.semaphore_signal(bar, inc=1, device_id={"mic": peer, "tm": tm}, device_id_type=MESH)

    @pl.when(tm < ntm - 1)
    def _():
        for peer in (mic, other):
            pl.semaphore_signal(bar, inc=1, device_id={"mic": peer, "tm": tm + 1}, device_id_type=MESH)

    loads = [
        pltpu.make_async_copy(fraction, fwraw.at[0], lsem.at[0]),
        pltpu.make_async_copy(weight, fwraw.at[1], lsem.at[1]),
        pltpu.make_async_copy(delay.at[0], raw.at[0], lsem.at[2]),
        pltpu.make_async_copy(signal, sig.at[:, pl.ds(0, TIME)], lsem.at[3]),
        pltpu.make_async_copy(delay.at[pl.ds(1, NB - 1)], raw.at[pl.ds(1, NB - 1)], lsem.at[4]),
    ]
    for c in loads:
        c.start()

    @pl.when(tm == ntm - 1)
    def _():
        sig[:, pl.ds(TIME, 128)] = jnp.zeros((MICS, 128), BF)
        psig[:, pl.ds(TIME, 128)] = jnp.zeros((MICS, 128), BF)

    def remote(src, dst, send, recv, **to):
        return pltpu.make_async_remote_copy(src, dst, send, recv, device_id={"mic": mic, "tm": tm, **to}, device_id_type=MESH)

    def send_fw():
        return remote(fw.at[1 - h], pfw, gs, gr, mic=other)

    def send_delay(b):
        return remote(dly.at[1 - h, b], pdly.at[b], ds_.at[b], dr.at[b], mic=other)

    def send_piece(c):
        cols = pl.ds(pl.multiple_of(c * SUB, 128), SUB)
        return remote(sig.at[:, cols], psig.at[:, cols], xs.at[c], xr.at[c], mic=other)

    def send_halo(k):
        dst = (sig, psig)[k]
        peer = (mic, other)[k]
        return remote(sig.at[:, pl.ds(0, 128)], dst.at[:, pl.ds(TIME, 128)], hs.at[k], hr.at[k], mic=peer, tm=tm - 1)

    def wait_halo(k):
        dst = (sig, psig)[k]
        remote(sig.at[:, pl.ds(0, 128)], dst.at[:, pl.ds(TIME, 128)], hs.at[k], hr.at[k]).wait_recv()

    loads[0].wait()
    loads[1].wait()
    for k in range(2):
        def put(half, i, v, k=k):
            fw[half, k, :, pl.ds(i * 128, 128)] = v
        halves(lambda i, k=k: fwraw[k, :, pl.ds(i * 128, 128)], put)

    def compact(b):
        def put(half, i, v):
            dly[half, b, :, pl.ds(i * 128, 128)] = v.astype(I16)
        halves(lambda i: raw[b, :, pl.ds(i * 128, 128)], put)

    loads[2].wait()
    compact(0)
    loads[3].wait()

    @pl.when(tm > 0)
    def _():
        pl.semaphore_wait(bar, 5)

    @pl.when(tm == 0)
    def _():
        pl.semaphore_wait(bar, 3)

    send_fw().start()
    send_delay(0).start()
    send_piece(0).start()
    send_piece(1).start()

    @pl.when(tm > 0)
    def _():
        send_halo(0).start()
        send_halo(1).start()

    loads[4].wait()

    @pl.loop(1, NB)
    def _(b):
        compact(b)
        send_delay(b).start()

        @pl.when(b < NB - 1)
        def _():
            send_piece(b + 1).start()

    fill_taps(fw.at[h], taps)

    @pl.loop(0, NB)
    def _(b):
        @pl.when((b == NB - 1) & (tm < ntm - 1))
        def _():
            wait_halo(0)

        spread(sig, b, g, hh)
        own[b] = block_dot(hh, taps, dly.at[h, b])

    send_fw().wait_recv()
    fill_taps(pfw, ptaps)
    send_piece(0).wait_recv()

    lane = lax.broadcasted_iota(jnp.int32, (128, 128), 1)

    def message(b, way, hop):
        peer = (right, left)[way]
        return remote(sbuf.at[way, b, hop], rbuf.at[way, b, hop], ss.at[way, b, hop], rs.at[way, b, hop], mic=peer)

    def length(odd, way):
        return 4 if odd == way else 3

    def hop(pair, k):
        for odd in range(2):
            for way in range(2):
                steps = length(odd, way)
                if k >= steps:
                    continue
                b = 2 * pair + odd
                ahead = steps - k
                dest = lax.rem(z + (ahead if way == 0 else RING - ahead), RING)
                total = part[b, dest]
                if k > 0:
                    message(b, way, k - 1).wait_recv()
                    total = total + rbuf[way, b, k - 1].astype(F32)
                sbuf[way, b, k] = total.astype(BF)
                message(b, way, k).start()

    def finish(pair):
        for odd in range(2):
            b = 2 * pair + odd
            total = part[b, z]
            for way in range(2):
                last = length(odd, way) - 1
                message(b, way, last).wait_recv()
                total = total + rbuf[way, b, last].astype(F32)
            flat = total.T
            start = pl.multiple_of(b * SUB, 128)
            out[:, pl.ds(start, 128)] = flat[0:64, :]
            out[:, pl.ds(pl.multiple_of(start + 128, 128), 128)] = flat[64:128, :]

    def form(b):
        spread(psig, b, g, hh)
        r = own[b] + block_dot(hh, ptaps, pdly.at[b])
        for i in range(4):
            top, bottom = r[0:128, i * 128 : i * 128 + 128], r[128:256, i * 128 : i * 128 + 128]
            part[b, 2 * i] = jnp.where(lane < 64, top, pltpu.roll(bottom, 64, 1))
            part[b, 2 * i + 1] = jnp.where(lane < 64, pltpu.roll(top, 64, 1), bottom)

    @pl.loop(0, 8)
    def _(i):
        @pl.when(i < 4)
        def _():
            send_delay(2 * i).wait_recv()
            send_piece(2 * i + 1).wait_recv()
            form(2 * i)
            send_delay(2 * i + 1).wait_recv()

            @pl.when(i < 3)
            def _():
                send_piece(2 * i + 2).wait_recv()

            @pl.when((i == 3) & (tm < ntm - 1))
            def _():
                wait_halo(1)

            form(2 * i + 1)
            hop(i, 0)

        for k in (3, 2, 1):
            @pl.when((i >= k) & (i < 4 + k))
            def _(k=k):
                hop(i - k, k)

        @pl.when(i >= 4)
        def _():
            finish(i - 4)

    send_fw().wait_send()

    @pl.loop(0, NB)
    def _(b):
        send_delay(b).wait_send()
        send_piece(b).wait_send()

    @pl.when(tm > 0)
    def _():
        send_halo(0).wait_send()
        send_halo(1).wait_send()

    @pl.loop(0, NB // 2)
    def _(i):
        for odd in range(2):
            for way in range(2):
                for k in range(length(odd, way)):
                    message(2 * i + odd, way, k).wait_send()


def shards(signal, delay, fraction, weight):
    dma = pltpu.SemaphoreType.DMA
    return pl.pallas_call(
        kernel,
        out_shape=jax.ShapeDtypeStruct((FOCUS // 16, TIME), F32),
        in_specs=[pl.BlockSpec(memory_space=pl.ANY)] * 4,
        out_specs=pl.BlockSpec(memory_space=pltpu.VMEM),
        scratch_shapes=[
            pltpu.VMEM((MICS, WIDE), BF),
            pltpu.VMEM((MICS, WIDE), BF),
            pltpu.VMEM((NB, MICS, FOCUS), jnp.int32),
            pltpu.VMEM((2, NB, MICS, HALF), I16),
            pltpu.VMEM((NB, MICS, HALF), I16),
            pltpu.VMEM((2, MICS, FOCUS), F32),
            pltpu.VMEM((2, 2, MICS, HALF), F32),
            pltpu.VMEM((2, MICS, HALF), F32),
            pltpu.VMEM((8, MICS, HALF), BF),
            pltpu.VMEM((8, MICS, HALF), BF),
            pltpu.VMEM((384, 128), F32),
            pltpu.VMEM((304, 512), BF),
            pltpu.VMEM((NB, SUB, HALF), F32),
            pltpu.VMEM((NB, RING, 128, 128), F32),
            pltpu.VMEM((2, NB, 4, 128, 128), BF),
            pltpu.VMEM((2, NB, 4, 128, 128), BF),
            dma((5,)),
            dma((NB,)), dma((NB,)),
            dma((NB,)), dma((NB,)),
            dma, dma,
            dma((2,)), dma((2,)),
            dma((2, NB, 4)), dma((2, NB, 4)),
        ],
        compiler_params=pltpu.CompilerParams(
            collective_id=0, has_side_effects=True, vmem_limit_bytes=48 * 1024 * 1024
        ),
    )(signal, delay, fraction, weight)


def solution(mesh):
    return jax.shard_map(
        shards,
        mesh=mesh,
        in_specs=(P("mic", "tm"), P("tm", "mic", None), P("mic", None), P("mic", None)),
        out_specs=P("mic", "tm"),
        check_vma=False,
    )
```

profile of v0, /device:TPU:8, one launch (start us, length us, event | category | flops | bytes accessed | tf_op | source)
XLA Modules:
  0.0 53.9 jit_solution(13064737448102463452)
XLA Ops:
  0.0 0.0 copy-start
  0.0 1.2 %copy-done = s32[8,32,1024]{2,1,0:T(8,128)S(1)} copy-done((s32[8,32,1024]{2,1,0:T(8,128)S(1)}, s32[8,32,1024]{2,1,0:T(8,128)}, u32[]{:S(2)}) %copy-start) | copy-done | bytes 1048600
  1.2 0.0 copy-start.1
  1.2 0.9 %copy-done.1 = bf16[32,2048]{1,0:T(8,128)(2,1)S(1)} copy-done((bf16[32,2048]{1,0:T(8,128)(2,1)S(1)}, bf16[32,2048]{1,0:T(8,128)(2,1)}, u32[]{:S(2)}) %copy-start.1) | copy-done | bytes 131096
  2.1 0.0 copy-start.2
  2.1 0.9 %copy-done.2 = f32[32,1024]{1,0:T(8,128)S(1)} copy-done((f32[32,1024]{1,0:T(8,128)S(1)}, f32[32,1024]{1,0:T(8,128)}, u32[]{:S(2)}) %copy-start.2) | copy-done | bytes 131096
  3.0 0.0 copy-start.3
  3.0 0.9 %copy-done.3 = f32[32,1024]{1,0:T(8,128)S(1)} copy-done((f32[32,1024]{1,0:T(8,128)S(1)}, f32[32,1024]{1,0:T(8,128)}, u32[]{:S(2)}) %copy-start.3) | copy-done | bytes 131096
  3.9 49.2 %shard_map.46 = f32[64,2048]{1,0:T(8,128)S(1)} custom-call(bf16[32,2048]{1,0:T(8,128)(2,1)S(1)} %copy-done.1, s32[8,32,1024]{2,1,0:T(8,128)S(1)} %copy-done, f32[32,1024]{1,0:T(8,128)S(1)} %copy-done.2, f32[32,1024]{1,0:T(8,128)S(1)} %copy-done.3), custom_call_target="tpu_custom_call" | custom-call | tf_op jit(solution)/shard_map/pallas_call | solution.py:314
  53.1 0.8 %copy.6 = f32[64,2048]{1,0:T(8,128)} copy(f32[64,2048]{1,0:T(8,128)S(1)} %shard_map.46) | data formatting | bytes 1048576
Async XLA Ops:
  0.0 1.2 %copy-start = (s32[8,32,1024]{2,1,0:T(8,128)S(1)}, s32[8,32,1024]{2,1,0:T(8,128)}, u32[]{:S(2)}) copy-start(s32[8,32,1024]{2,1,0:T(8,128)} %delay.1) | copy-start | bytes 3145732
  1.2 0.9 %copy-start.1 = (bf16[32,2048]{1,0:T(8,128)(2,1)S(1)}, bf16[32,2048]{1,0:T(8,128)(2,1)}, u32[]{:S(2)}) copy-start(bf16[32,2048]{1,0:T(8,128)(2,1)} %signal.1) | copy-start | bytes 393220
  2.1 0.9 %copy-start.2 = (f32[32,1024]{1,0:T(8,128)S(1)}, f32[32,1024]{1,0:T(8,128)}, u32[]{:S(2)}) copy-start(f32[32,1024]{1,0:T(8,128)} %fraction.1) | copy-start | bytes 393220
  3.0 0.9 %copy-start.3 = (f32[32,1024]{1,0:T(8,128)S(1)}, f32[32,1024]{1,0:T(8,128)}, u32[]{:S(2)}) copy-start(f32[32,1024]{1,0:T(8,128)} %weight.1) | copy-start | bytes 393220
where the time goes:
time: 54.1 us; the launch traced here: 53.9 us
  Pallas kernels  49.2 us (91%)
  local copies, waits for them, and re-layouts  4.73 us (9%)
    pallas_call x1, Pallas kernels, shards(): pl.pallas_call(kernel, out_shape=jax.ShapeDtypeStruct((FOCUS // 16, TIME)...  49.2 us
    unnamed x9, local copies, waits for them, and re-layouts  4.73 us

commit v1 on v0

--- a/solution.py
+++ b/solution.py
@@ -64,29 +64,31 @@
             rows, cols = tile(mh, fc)
             t = [taps[p, rows, cols] for p in range(8)]
             d = delay[rows, cols]
-            at = [(d + I16(7 - q)) >> I16(3) for q in range(8)]
+            row, column = (d >> I16(3)).astype(BF), (d & I16(7)).astype(BF)
+            after = row + BF(1)
+            at = [jnp.where(column > BF(q), after, row) for q in range(8)]
             for bit in (4, 2, 1):
-                on = (d & I16(bit)) != I16(0)
+                on = (d & I16(bit)).astype(BF) != BF(0)
                 t = [jnp.where(on, t[(q - bit) % 8], t[q]) for q in range(8)]
             parts.append((t, at))
         columns.append(
             jnp.concatenate(
-                [jnp.where(at[q] == I16(h), t[q], zero) for h in range(8) for q in range(8) for t, at in parts],
+                [jnp.where(at[q] == BF(h), t[q], zero) for h in range(8) for q in range(8) for t, at in parts],
                 axis=0,
             )
         )
     return jnp.concatenate(columns, axis=1)
 
 
-def spread(sig, b, g, hh):
-    s = sig[:, pl.ds(pl.multiple_of(b * SUB, 128), 384)].astype(F32)
-    g[...] = jnp.concatenate([s] + [pltpu.roll(s, 384 - k, 1) for k in range(1, 4)], axis=0).T
+def spread(sig, pair, g, hh):
+    s = sig[:, pl.ds(pl.multiple_of(pair * 2 * SUB, 128), 640)].astype(F32)
+    g[...] = jnp.concatenate([s] + [pltpu.roll(s, 640 - k, 1) for k in range(1, 4)], axis=0).T
     for k in range(4):
-        hh[:, pl.ds(k * 128, 128)] = g[pl.ds(4 * k, 304), :].astype(BF)
-
-
-def block_dot(hh, taps, delay):
-    lhs = jnp.concatenate([hh[pl.ds(16 * k, SUB), :] for k in range(4)], axis=1)
+        hh[:, pl.ds(k * 128, 128)] = g[pl.ds(4 * k, 2 * SUB + 48), :].astype(BF)
+
+
+def block_dot(hh, odd, taps, delay):
+    lhs = jnp.concatenate([hh[pl.ds(SUB * odd + 16 * k, SUB), :] for k in range(4)], axis=1)
     return jnp.dot(lhs, coefficients(taps, delay), preferred_element_type=F32)
 
 
@@ -109,8 +111,10 @@
     ntm = lax.axis_size("tm")
 
     bar = pltpu.get_barrier_semaphore()
-    for peer in (other, right, left):
-        pl.semaphore_signal(bar, inc=1, device_id={"mic": peer, "tm": tm}, device_id_type=MESH)
+    core = lax.rem(tm, 2)
+    sibling = tm + 1 - 2 * core
+    for peer, at in ((other, tm), (right, tm), (left, tm), (mic, sibling)):
+        pl.semaphore_signal(bar, inc=1, device_id={"mic": peer, "tm": at}, device_id_type=MESH)
 
     @pl.when(tm < ntm - 1)
     def _():
@@ -136,7 +140,10 @@
         return pltpu.make_async_remote_copy(src, dst, send, recv, device_id={"mic": mic, "tm": tm, **to}, device_id_type=MESH)
 
     def send_fw():
-        return remote(fw.at[1 - h], pfw, gs, gr, mic=other)
+        return remote(fw.at[1 - h, core], pfw.at[core], gs.at[0], gr.at[0], mic=other)
+
+    def share_fw():
+        return remote(pfw.at[core], pfw.at[core], gs.at[1], gr.at[1], tm=sibling)
 
     def send_delay(b):
         return remote(dly.at[1 - h, b], pdly.at[b], ds_.at[b], dr.at[b], mic=other)
@@ -172,22 +179,16 @@
 
     @pl.when(tm > 0)
     def _():
-        pl.semaphore_wait(bar, 5)
+        pl.semaphore_wait(bar, 6)
 
     @pl.when(tm == 0)
     def _():
-        pl.semaphore_wait(bar, 3)
+        pl.semaphore_wait(bar, 4)
 
     send_fw().start()
     send_delay(0).start()
     send_piece(0).start()
     send_piece(1).start()
-
-    @pl.when(tm > 0)
-    def _():
-        send_halo(0).start()
-        send_halo(1).start()
-
     loads[4].wait()
 
     @pl.loop(1, NB)
@@ -199,18 +200,29 @@
         def _():
             send_piece(b + 1).start()
 
+        @pl.when((b == 2) & (tm > 0))
+        def _():
+            send_halo(0).start()
+            send_halo(1).start()
+
     fill_taps(fw.at[h], taps)
 
-    @pl.loop(0, NB)
-    def _(b):
-        @pl.when((b == NB - 1) & (tm < ntm - 1))
+    @pl.loop(0, NB // 2)
+    def _(i):
+        @pl.when((i == NB // 2 - 1) & (tm < ntm - 1))
         def _():
             wait_halo(0)
 
-        spread(sig, b, g, hh)
-        own[b] = block_dot(hh, taps, dly.at[h, b])
-
-    send_fw().wait_recv()
+        @pl.when(i == 2)
+        def _():
+            send_fw().wait_recv()
+            share_fw().start()
+
+        spread(sig, i, g, hh)
+        for odd in range(2):
+            own[2 * i + odd] = block_dot(hh, odd, taps, dly.at[h, 2 * i + odd])
+
+    share_fw().wait_recv()
     fill_taps(pfw, ptaps)
     send_piece(0).wait_recv()
 
@@ -252,44 +264,54 @@
             out[:, pl.ds(start, 128)] = flat[0:64, :]
             out[:, pl.ds(pl.multiple_of(start + 128, 128), 128)] = flat[64:128, :]
 
-    def form(b):
-        spread(psig, b, g, hh)
-        r = own[b] + block_dot(hh, ptaps, pdly.at[b])
-        for i in range(4):
-            top, bottom = r[0:128, i * 128 : i * 128 + 128], r[128:256, i * 128 : i * 128 + 128]
-            part[b, 2 * i] = jnp.where(lane < 64, top, pltpu.roll(bottom, 64, 1))
-            part[b, 2 * i + 1] = jnp.where(lane < 64, pltpu.roll(top, 64, 1), bottom)
-
-    @pl.loop(0, 8)
-    def _(i):
-        @pl.when(i < 4)
-        def _():
-            send_delay(2 * i).wait_recv()
-            send_piece(2 * i + 1).wait_recv()
-            form(2 * i)
-            send_delay(2 * i + 1).wait_recv()
-
-            @pl.when(i < 3)
-            def _():
-                send_piece(2 * i + 2).wait_recv()
-
-            @pl.when((i == 3) & (tm < ntm - 1))
-            def _():
-                wait_halo(1)
-
-            form(2 * i + 1)
-            hop(i, 0)
-
-        for k in (3, 2, 1):
-            @pl.when((i >= k) & (i < 4 + k))
-            def _(k=k):
-                hop(i - k, k)
-
-        @pl.when(i >= 4)
-        def _():
-            finish(i - 4)
+    def form(pair):
+        spread(psig, pair, g, hh)
+        for odd in range(2):
+            b = 2 * pair + odd
+            r = own[b] + block_dot(hh, odd, ptaps, pdly.at[b])
+            for i in range(4):
+                top, bottom = r[0:128, i * 128 : i * 128 + 128], r[128:256, i * 128 : i * 128 + 128]
+                part[b, 2 * i] = jnp.where(lane < 64, top, pltpu.roll(bottom, 64, 1))
+                part[b, 2 * i + 1] = jnp.where(lane < 64, pltpu.roll(top, 64, 1), bottom)
+
+    @pl.loop(0, NB // 2)
+    def _(i):
+        send_delay(2 * i).wait_recv()
+        send_piece(2 * i + 1).wait_recv()
+        send_delay(2 * i + 1).wait_recv()
+
+        @pl.when(i < NB // 2 - 1)
+        def _():
+            send_piece(2 * i + 2).wait_recv()
+
+        @pl.when((i == NB // 2 - 1) & (tm < ntm - 1))
+        def _():
+            wait_halo(1)
+
+        form(i)
+        hop(i, 0)
+
+        @pl.when(i > 0)
+        def _():
+            hop(i - 1, 1)
+
+    hop(0, 2)
+    hop(3, 1)
+
+    @pl.loop(1, NB // 2)
+    def _(i):
+        hop(i, 2)
+
+    @pl.loop(0, NB // 2)
+    def _(i):
+        hop(i, 3)
+
+    @pl.loop(0, NB // 2)
+    def _(i):
+        finish(i)
 
     send_fw().wait_send()
+    share_fw().wait_send()
 
     @pl.loop(0, NB)
     def _(b):
@@ -314,7 +336,7 @@
     return pl.pallas_call(
         kernel,
         out_shape=jax.ShapeDtypeStruct((FOCUS // 16, TIME), F32),
-        in_specs=[pl.BlockSpec(memory_space=pl.ANY)] * 4,
+        in_specs=[pl.BlockSpec(memory_space=pltpu.HBM)] * 4,
         out_specs=pl.BlockSpec(memory_space=pltpu.VMEM),
         scratch_shapes=[
             pltpu.VMEM((MICS, WIDE), BF),
@@ -327,8 +349,8 @@
             pltpu.VMEM((2, MICS, HALF), F32),
             pltpu.VMEM((8, MICS, HALF), BF),
             pltpu.VMEM((8, MICS, HALF), BF),
-            pltpu.VMEM((384, 128), F32),
-            pltpu.VMEM((304, 512), BF),
+            pltpu.VMEM((640, 128), F32),
+            pltpu.VMEM((2 * SUB + 48, 512), BF),
             pltpu.VMEM((NB, SUB, HALF), F32),
             pltpu.VMEM((NB, RING, 128, 128), F32),
             pltpu.VMEM((2, NB, 4, 128, 128), BF),
@@ -336,12 +358,12 @@
             dma((5,)),
             dma((NB,)), dma((NB,)),
             dma((NB,)), dma((NB,)),
-            dma, dma,
+            dma((2,)), dma((2,)),
             dma((2,)), dma((2,)),
             dma((2, NB, 4)), dma((2, NB, 4)),
         ],
         compiler_params=pltpu.CompilerParams(
-            collective_id=0, has_side_effects=True, vmem_limit_bytes=48 * 1024 * 1024
+            collective_id=0, has_side_effects=True, vmem_limit_bytes=60 * 1024 * 1024
         ),
     )(signal, delay, fraction, weight)
 

time: 54.1 us -> 46.2 us (0.85); the launches traced: 53.9 us -> 45.4 us
  Pallas kernels: 49.2 us -> 43.5 us
  local copies, waits for them, and re-layouts: 4.73 us -> 1.87 us
    pallas_call x1, Pallas kernels: 49.2 us -> 43.5 us  [shards(): pl.pallas_call(kernel, out_shape=jax.ShapeDtypeStruct((FOCUS // 16, TIME)...]
    unnamed x9 -> x1, local copies, waits for them, and re-layouts: 4.73 us -> 1.87 us
where the time goes in v1:
time: 46.2 us; the launch traced here: 45.4 us
  Pallas kernels  43.5 us (94%)
  local copies, waits for them, and re-layouts  1.87 us (4%)
    pallas_call x1, Pallas kernels, shards(): pl.pallas_call(kernel, out_shape=jax.ShapeDtypeStruct((FOCUS // 16, TIME)...  43.5 us
    unnamed x1, local copies, waits for them, and re-layouts  1.87 us

profile of v1, /device:TPU:8, one launch (start us, length us, event | category | flops | bytes accessed | tf_op | source)
XLA Modules:
  0.0 45.4 jit_solution(7931417278008971214)
XLA Ops:
  0.0 43.5 %shard_map.46 = f32[64,2048]{1,0:T(8,128)} custom-call(bf16[32,2048]{1,0:T(8,128)(2,1)} %signal.1, s32[8,32,1024]{2,1,0:T(8,128)} %delay.1, f32[32,1024]{1,0:T(8,128)} %fraction.1, f32[32,1024]{1,0:T(8,128)} %weight.1), custom_call_target="tpu_custom_call" | custom-call | tf_op jit(solution)/shard_map/pallas_call | solution.py:336
  43.5 1.9 %copy.6 = f32[64,2048]{1,0:T(8,128)} copy(f32[64,2048]{1,0:T(8,128)} %shard_map.46) | data formatting | bytes 1048576

commit v2 on v1

--- a/solution.py
+++ b/solution.py
@@ -80,11 +80,13 @@
     return jnp.concatenate(columns, axis=1)
 
 
-def spread(sig, pair, g, hh):
-    s = sig[:, pl.ds(pl.multiple_of(pair * 2 * SUB, 128), 640)].astype(F32)
-    g[...] = jnp.concatenate([s] + [pltpu.roll(s, 640 - k, 1) for k in range(1, 4)], axis=0).T
+def spread(sig, first, blocks, g, hh):
+    wide = SUB * blocks + 128
+    s = sig[:, pl.ds(pl.multiple_of(first * SUB, 128), wide)].astype(F32)
+    g[pl.ds(0, wide), :] = jnp.concatenate([s] + [pltpu.roll(s, wide - k, 1) for k in range(1, 4)], axis=0).T
+    rows = SUB * blocks + 48
     for k in range(4):
-        hh[:, pl.ds(k * 128, 128)] = g[pl.ds(4 * k, 2 * SUB + 48), :].astype(BF)
+        hh[pl.ds(0, rows), pl.ds(k * 128, 128)] = g[pl.ds(4 * k, rows), :].astype(BF)
 
 
 def block_dot(hh, odd, taps, delay):
@@ -101,7 +103,7 @@
 
 
 def kernel(signal, delay, fraction, weight, out,
-           sig, psig, raw, dly, pdly, fwraw, fw, pfw, taps, ptaps, g, hh, own, part, sbuf, rbuf,
+           sig, psig, raw, dly, pdly, fwraw, fw, pfw, taps, ptaps, g, hh, own, part, sbuf, rbuf, outv,
            lsem, xs, xr, ds_, dr, gs, gr, hs, hr, ss, rs):
     mic, tm = lax.axis_index("mic"), lax.axis_index("tm")
     z, h = mic // 2, lax.rem(mic, 2)
@@ -191,8 +193,7 @@
     send_piece(1).start()
     loads[4].wait()
 
-    @pl.loop(1, NB)
-    def _(b):
+    def pass_on(b):
         compact(b)
         send_delay(b).start()
 
@@ -200,28 +201,30 @@
         def _():
             send_piece(b + 1).start()
 
-        @pl.when((b == 2) & (tm > 0))
-        def _():
-            send_halo(0).start()
-            send_halo(1).start()
+    pass_on(1)
+    pass_on(2)
+
+    @pl.when(tm > 0)
+    def _():
+        send_halo(0).start()
+        send_halo(1).start()
 
     fill_taps(fw.at[h], taps)
 
-    @pl.loop(0, NB // 2)
-    def _(i):
-        @pl.when((i == NB // 2 - 1) & (tm < ntm - 1))
-        def _():
-            wait_halo(0)
-
-        @pl.when(i == 2)
-        def _():
-            send_fw().wait_recv()
-            share_fw().start()
-
-        spread(sig, i, g, hh)
-        for odd in range(2):
-            own[2 * i + odd] = block_dot(hh, odd, taps, dly.at[h, 2 * i + odd])
-
+    def half(pair):
+        spread(sig, 2 * pair, 2, g, hh)
+        for odd in range(2):
+            own[2 * pair + odd] = block_dot(hh, odd, taps, dly.at[h, 2 * pair + odd])
+
+    @pl.loop(0, 2)
+    def _(i):
+        half(i)
+        pass_on(2 * i + 3)
+        pass_on(2 * i + 4)
+
+    send_fw().wait_recv()
+    share_fw().start()
+    pass_on(NB - 1)
     share_fw().wait_recv()
     fill_taps(pfw, ptaps)
     send_piece(0).wait_recv()
@@ -235,21 +238,24 @@
     def length(odd, way):
         return 4 if odd == way else 3
 
-    def hop(pair, k):
-        for odd in range(2):
-            for way in range(2):
-                steps = length(odd, way)
-                if k >= steps:
-                    continue
-                b = 2 * pair + odd
-                ahead = steps - k
-                dest = lax.rem(z + (ahead if way == 0 else RING - ahead), RING)
-                total = part[b, dest]
-                if k > 0:
-                    message(b, way, k - 1).wait_recv()
-                    total = total + rbuf[way, b, k - 1].astype(F32)
-                sbuf[way, b, k] = total.astype(BF)
-                message(b, way, k).start()
+    def hop(pair, odd, k):
+        for way in range(2):
+            steps = length(odd, way)
+            if k >= steps:
+                continue
+            b = 2 * pair + odd
+            ahead = steps - k
+            dest = lax.rem(z + (ahead if way == 0 else RING - ahead), RING)
+            total = part[b, dest]
+            if k > 0:
+                message(b, way, k - 1).wait_recv()
+                total = total + rbuf[way, b, k - 1].astype(F32)
+            sbuf[way, b, k] = total.astype(BF)
+            message(b, way, k).start()
+
+    def deliver(b):
+        cols = pl.ds(pl.multiple_of(b * SUB, 128), SUB)
+        return pltpu.make_async_copy(outv.at[:, cols], out.at[:, cols], lsem.at[5 + b])
 
     def finish(pair):
         for odd in range(2):
@@ -261,50 +267,76 @@
                 total = total + rbuf[way, b, last].astype(F32)
             flat = total.T
             start = pl.multiple_of(b * SUB, 128)
-            out[:, pl.ds(start, 128)] = flat[0:64, :]
-            out[:, pl.ds(pl.multiple_of(start + 128, 128), 128)] = flat[64:128, :]
-
-    def form(pair):
-        spread(psig, pair, g, hh)
-        for odd in range(2):
-            b = 2 * pair + odd
+            outv[:, pl.ds(start, 128)] = flat[0:64, :]
+            outv[:, pl.ds(pl.multiple_of(start + 128, 128), 128)] = flat[64:128, :]
+            deliver(b).start()
+
+    def form(first, blocks):
+        spread(psig, first, blocks, g, hh)
+        for odd in range(blocks):
+            b = first + odd
             r = own[b] + block_dot(hh, odd, ptaps, pdly.at[b])
             for i in range(4):
                 top, bottom = r[0:128, i * 128 : i * 128 + 128], r[128:256, i * 128 : i * 128 + 128]
                 part[b, 2 * i] = jnp.where(lane < 64, top, pltpu.roll(bottom, 64, 1))
                 part[b, 2 * i + 1] = jnp.where(lane < 64, pltpu.roll(top, 64, 1), bottom)
 
-    @pl.loop(0, NB // 2)
-    def _(i):
+    last = NB // 2 - 1
+
+    @pl.loop(0, 2)
+    def _(b):
+        send_delay(b).wait_recv()
+        send_piece(b + 1).wait_recv()
+        form(b, 1)
+
+        for odd in range(2):
+            @pl.when(b == odd)
+            def _(odd=odd):
+                hop(0, odd, 0)
+
+    @pl.loop(1, NB // 2)
+    def _(i):
+        @pl.when((i == last) & (tm < ntm - 1))
+        def _():
+            wait_halo(0)
+
+        @pl.when(i >= 2)
+        def _():
+            half(i)
+            for odd in range(2):
+                hop(i - 2, odd, 1)
+
         send_delay(2 * i).wait_recv()
         send_piece(2 * i + 1).wait_recv()
         send_delay(2 * i + 1).wait_recv()
 
-        @pl.when(i < NB // 2 - 1)
+        @pl.when(i < last)
         def _():
             send_piece(2 * i + 2).wait_recv()
 
-        @pl.when((i == NB // 2 - 1) & (tm < ntm - 1))
+        @pl.when((i == last) & (tm < ntm - 1))
         def _():
             wait_halo(1)
 
-        form(i)
-        hop(i, 0)
-
-        @pl.when(i > 0)
-        def _():
-            hop(i - 1, 1)
-
-    hop(0, 2)
-    hop(3, 1)
+        form(2 * i, 2)
+        for odd in range(2):
+            hop(i, odd, 0)
+    for odd in range(2):
+        hop(last - 1, odd, 1)
+    for odd in range(2):
+        hop(0, odd, 2)
+    for odd in range(2):
+        hop(last, odd, 1)
 
     @pl.loop(1, NB // 2)
     def _(i):
-        hop(i, 2)
+        for odd in range(2):
+            hop(i, odd, 2)
 
     @pl.loop(0, NB // 2)
     def _(i):
-        hop(i, 3)
+        for odd in range(2):
+            hop(i, odd, 3)
 
     @pl.loop(0, NB // 2)
     def _(i):
@@ -329,6 +361,7 @@
             for way in range(2):
                 for k in range(length(odd, way)):
                     message(2 * i + odd, way, k).wait_send()
+            deliver(2 * i + odd).wait()
 
 
 def shards(signal, delay, fraction, weight):
@@ -337,7 +370,7 @@
         kernel,
         out_shape=jax.ShapeDtypeStruct((FOCUS // 16, TIME), F32),
         in_specs=[pl.BlockSpec(memory_space=pltpu.HBM)] * 4,
-        out_specs=pl.BlockSpec(memory_space=pltpu.VMEM),
+        out_specs=pl.BlockSpec(memory_space=pltpu.HBM),
         scratch_shapes=[
             pltpu.VMEM((MICS, WIDE), BF),
             pltpu.VMEM((MICS, WIDE), BF),
@@ -355,7 +388,8 @@
             pltpu.VMEM((NB, RING, 128, 128), F32),
             pltpu.VMEM((2, NB, 4, 128, 128), BF),
             pltpu.VMEM((2, NB, 4, 128, 128), BF),
-            dma((5,)),
+            pltpu.VMEM((FOCUS // 16, TIME), F32),
+            dma((5 + NB,)),
             dma((NB,)), dma((NB,)),
             dma((NB,)), dma((NB,)),
             dma((2,)), dma((2,)),

time: 46.2 us -> 44.2 us (0.957); the launches traced: 45.4 us -> 44 us
  Pallas kernels: 43.5 us -> 42.1 us
    pallas_call x1, Pallas kernels: 43.5 us -> 42.1 us  [shards(): pl.pallas_call(kernel, out_shape=jax.ShapeDtypeStruct((FOCUS // 16, TIME)...]
where the time goes in v2:
time: 44.2 us; the launch traced here: 44 us
  Pallas kernels  42.1 us (95%)
  local copies, waits for them, and re-layouts  1.87 us (4%)
    pallas_call x1, Pallas kernels, shards(): pl.pallas_call(kernel, out_shape=jax.ShapeDtypeStruct((FOCUS // 16, TIME)...  42.1 us
    unnamed x1, local copies, waits for them, and re-layouts  1.87 us

profile of v2, /device:TPU:8, one launch (start us, length us, event | category | flops | bytes accessed | tf_op | source)
XLA Modules:
  0.0 44.0 jit_solution(9031160509339545457)
XLA Ops:
  0.0 42.1 %shard_map.46 = f32[64,2048]{1,0:T(8,128)} custom-call(bf16[32,2048]{1,0:T(8,128)(2,1)} %signal.1, s32[8,32,1024]{2,1,0:T(8,128)} %delay.1, f32[32,1024]{1,0:T(8,128)} %fraction.1, f32[32,1024]{1,0:T(8,128)} %weight.1), custom_call_target="tpu_custom_call" | custom-call | tf_op jit(solution)/shard_map/pallas_call | solution.py:369
  42.2 1.9 %copy.6 = f32[64,2048]{1,0:T(8,128)} copy(f32[64,2048]{1,0:T(8,128)} %shard_map.46) | data formatting | bytes 1048576

commit v3 on v2

--- a/solution.py
+++ b/solution.py
@@ -103,7 +103,7 @@
 
 
 def kernel(signal, delay, fraction, weight, out,
-           sig, psig, raw, dly, pdly, fwraw, fw, pfw, taps, ptaps, g, hh, own, part, sbuf, rbuf, outv,
+           sig, psig, raw, dly, pdly, fwraw, fw, pfw, taps, ptaps, g, hh, own, part, sbuf, rbuf,
            lsem, xs, xr, ds_, dr, gs, gr, hs, hr, ss, rs):
     mic, tm = lax.axis_index("mic"), lax.axis_index("tm")
     z, h = mic // 2, lax.rem(mic, 2)
@@ -188,19 +188,17 @@
         pl.semaphore_wait(bar, 4)
 
     send_fw().start()
-    send_delay(0).start()
     send_piece(0).start()
     send_piece(1).start()
+    send_delay(0).start()
     loads[4].wait()
 
     def pass_on(b):
+        if b < NB - 1:
+            send_piece(b + 1).start()
         compact(b)
         send_delay(b).start()
 
-        @pl.when(b < NB - 1)
-        def _():
-            send_piece(b + 1).start()
-
     pass_on(1)
     pass_on(2)
 
@@ -216,15 +214,12 @@
         for odd in range(2):
             own[2 * pair + odd] = block_dot(hh, odd, taps, dly.at[h, 2 * pair + odd])
 
-    @pl.loop(0, 2)
-    def _(i):
-        half(i)
-        pass_on(2 * i + 3)
-        pass_on(2 * i + 4)
-
+    half(0)
+    for b in range(3, NB):
+        pass_on(b)
     send_fw().wait_recv()
     share_fw().start()
-    pass_on(NB - 1)
+    half(1)
     share_fw().wait_recv()
     fill_taps(pfw, ptaps)
     send_piece(0).wait_recv()
@@ -253,10 +248,6 @@
             sbuf[way, b, k] = total.astype(BF)
             message(b, way, k).start()
 
-    def deliver(b):
-        cols = pl.ds(pl.multiple_of(b * SUB, 128), SUB)
-        return pltpu.make_async_copy(outv.at[:, cols], out.at[:, cols], lsem.at[5 + b])
-
     def finish(pair):
         for odd in range(2):
             b = 2 * pair + odd
@@ -267,12 +258,10 @@
                 total = total + rbuf[way, b, last].astype(F32)
             flat = total.T
             start = pl.multiple_of(b * SUB, 128)
-            outv[:, pl.ds(start, 128)] = flat[0:64, :]
-            outv[:, pl.ds(pl.multiple_of(start + 128, 128), 128)] = flat[64:128, :]
-            deliver(b).start()
+            out[:, pl.ds(start, 128)] = flat[0:64, :]
+            out[:, pl.ds(pl.multiple_of(start + 128, 128), 128)] = flat[64:128, :]
 
     def form(first, blocks):
-        spread(psig, first, blocks, g, hh)
         for odd in range(blocks):
             b = first + odd
             r = own[b] + block_dot(hh, odd, ptaps, pdly.at[b])
@@ -285,8 +274,9 @@
 
     @pl.loop(0, 2)
     def _(b):
+        send_piece(b + 1).wait_recv()
+        spread(psig, b, 1, g, hh)
         send_delay(b).wait_recv()
-        send_piece(b + 1).wait_recv()
         form(b, 1)
 
         for odd in range(2):
@@ -318,6 +308,7 @@
         def _():
             wait_halo(1)
 
+        spread(psig, 2 * i, 2, g, hh)
         form(2 * i, 2)
         for odd in range(2):
             hop(i, odd, 0)
@@ -361,16 +352,15 @@
             for way in range(2):
                 for k in range(length(odd, way)):
                     message(2 * i + odd, way, k).wait_send()
-            deliver(2 * i + odd).wait()
 
 
 def shards(signal, delay, fraction, weight):
     dma = pltpu.SemaphoreType.DMA
     return pl.pallas_call(
         kernel,
-        out_shape=jax.ShapeDtypeStruct((FOCUS // 16, TIME), F32),
+        out_shape=pltpu.VMEM((FOCUS // 16, TIME), F32),
         in_specs=[pl.BlockSpec(memory_space=pltpu.HBM)] * 4,
-        out_specs=pl.BlockSpec(memory_space=pltpu.HBM),
+        out_specs=pl.BlockSpec(memory_space=pltpu.VMEM),
         scratch_shapes=[
             pltpu.VMEM((MICS, WIDE), BF),
             pltpu.VMEM((MICS, WIDE), BF),
@@ -388,8 +378,7 @@
             pltpu.VMEM((NB, RING, 128, 128), F32),
             pltpu.VMEM((2, NB, 4, 128, 128), BF),
             pltpu.VMEM((2, NB, 4, 128, 128), BF),
-            pltpu.VMEM((FOCUS // 16, TIME), F32),
-            dma((5 + NB,)),
+            dma((5,)),
             dma((NB,)), dma((NB,)),
             dma((NB,)), dma((NB,)),
             dma((2,)), dma((2,)),
@@ -397,9 +386,9 @@
             dma((2, NB, 4)), dma((2, NB, 4)),
         ],
         compiler_params=pltpu.CompilerParams(
-            collective_id=0, has_side_effects=True, vmem_limit_bytes=60 * 1024 * 1024
+            collective_id=0, has_side_effects=True, vmem_limit_bytes=40 * 1024 * 1024
         ),
-    )(signal, delay, fraction, weight)
+    )(*(pltpu.with_memory_space_constraint(x, pltpu.HBM) for x in (signal, delay, fraction, weight)))
 
 
 def solution(mesh):

time: 44.2 us -> 42.5 us (0.962)
  local copies, waits for them, and re-layouts: 1.87 us -> 0.8 us
  Pallas kernels: 42.1 us -> 41.6 us
    unnamed x1, local copies, waits for them, and re-layouts: 1.87 us -> 0.8 us
    pallas_call x1, Pallas kernels: 42.1 us -> 41.6 us  [shards(): pl.pallas_call(kernel, out_shape=pltpu.VMEM((FOCUS // 16, TIME), F32), in...]
where the time goes in v3:
time: 42.5 us; the launch traced here: 42.4 us
  Pallas kernels  41.6 us (98%)
  local copies, waits for them, and re-layouts  0.8 us (2%)
    pallas_call x1, Pallas kernels, shards(): pl.pallas_call(kernel, out_shape=pltpu.VMEM((FOCUS // 16, TIME), F32), in...  41.6 us

profile of v3, /device:TPU:8, one launch (start us, length us, event | category | flops | bytes accessed | tf_op | source)
XLA Modules:
  0.0 42.4 jit_solution(18060556483750136040)
XLA Ops:
  0.0 41.6 %shard_map.46 = f32[64,2048]{1,0:T(8,128)S(1)} custom-call(bf16[32,2048]{1,0:T(8,128)(2,1)} %signal.1, s32[8,32,1024]{2,1,0:T(8,128)} %delay.1, f32[32,1024]{1,0:T(8,128)} %fraction.1, f32[32,1024]{1,0:T(8,128)} %weight.1), custom_call_target="tpu_custom_call" | custom-call | tf_op jit(solution)/shard_map/pallas_call | solution.py:359
  41.6 0.8 %copy.6 = f32[64,2048]{1,0:T(8,128)} copy(f32[64,2048]{1,0:T(8,128)S(1)} %shard_map.46) | data formatting | bytes 1048576

commit v4 on v3

--- a/solution.py
+++ b/solution.py
@@ -130,8 +130,8 @@
         pltpu.make_async_copy(signal, sig.at[:, pl.ds(0, TIME)], lsem.at[3]),
         pltpu.make_async_copy(delay.at[pl.ds(1, NB - 1)], raw.at[pl.ds(1, NB - 1)], lsem.at[4]),
     ]
-    for c in loads:
-        c.start()
+    for k in (3, 0, 1, 2, 4):
+        loads[k].start()
 
     @pl.when(tm == ntm - 1)
     def _():
@@ -163,12 +163,25 @@
         dst = (sig, psig)[k]
         remote(sig.at[:, pl.ds(0, 128)], dst.at[:, pl.ds(TIME, 128)], hs.at[k], hr.at[k]).wait_recv()
 
+    loads[3].wait()
+
+    @pl.when(tm > 0)
+    def _():
+        pl.semaphore_wait(bar, 6)
+
+    @pl.when(tm == 0)
+    def _():
+        pl.semaphore_wait(bar, 4)
+
+    send_piece(0).start()
+    send_piece(1).start()
     loads[0].wait()
     loads[1].wait()
     for k in range(2):
         def put(half, i, v, k=k):
             fw[half, k, :, pl.ds(i * 128, 128)] = v
         halves(lambda i, k=k: fwraw[k, :, pl.ds(i * 128, 128)], put)
+    send_fw().start()
 
     def compact(b):
         def put(half, i, v):
@@ -177,19 +190,6 @@
 
     loads[2].wait()
     compact(0)
-    loads[3].wait()
-
-    @pl.when(tm > 0)
-    def _():
-        pl.semaphore_wait(bar, 6)
-
-    @pl.when(tm == 0)
-    def _():
-        pl.semaphore_wait(bar, 4)
-
-    send_fw().start()
-    send_piece(0).start()
-    send_piece(1).start()
     send_delay(0).start()
     loads[4].wait()
 
@@ -293,8 +293,16 @@
         @pl.when(i >= 2)
         def _():
             half(i)
+
+        @pl.when(i == 2)
+        def _():
             for odd in range(2):
-                hop(i - 2, odd, 1)
+                hop(0, odd, 1)
+
+        @pl.when(i == 3)
+        def _():
+            for odd in range(2):
+                hop(0, odd, 2)
 
         send_delay(2 * i).wait_recv()
         send_piece(2 * i + 1).wait_recv()
@@ -312,24 +320,29 @@
         form(2 * i, 2)
         for odd in range(2):
             hop(i, odd, 0)
+
+        @pl.when(i == 2)
+        def _():
+            for odd in range(2):
+                hop(1, odd, 1)
+
     for odd in range(2):
-        hop(last - 1, odd, 1)
+        hop(2, odd, 1)
     for odd in range(2):
-        hop(0, odd, 2)
+        hop(1, odd, 2)
     for odd in range(2):
-        hop(last, odd, 1)
-
-    @pl.loop(1, NB // 2)
-    def _(i):
-        for odd in range(2):
-            hop(i, odd, 2)
+        hop(3, odd, 1)
+    for odd in range(2):
+        hop(2, odd, 2)
+    for odd in range(2):
+        hop(3, odd, 2)
 
     @pl.loop(0, NB // 2)
     def _(i):
         for odd in range(2):
             hop(i, odd, 3)
 
-    @pl.loop(0, NB // 2)
+    @pl.loop(0, last)
     def _(i):
         finish(i)
 
@@ -352,6 +365,8 @@
             for way in range(2):
                 for k in range(length(odd, way)):
                     message(2 * i + odd, way, k).wait_send()
+
+    finish(last)
 
 
 def shards(signal, delay, fraction, weight):

time: 42.5 us -> 42 us (0.988)
  Pallas kernels: 41.6 us -> 41.1 us
    pallas_call x1, Pallas kernels: 41.6 us -> 41.1 us  [shards(): pl.pallas_call(kernel, out_shape=pltpu.VMEM((FOCUS // 16, TIME), F32), in...]
where the time goes in v4:
time: 42 us; the launch traced here: 41.9 us
  Pallas kernels  41.1 us (98%)
  local copies, waits for them, and re-layouts  0.8 us (2%)
    pallas_call x1, Pallas kernels, shards(): pl.pallas_call(kernel, out_shape=pltpu.VMEM((FOCUS // 16, TIME), F32), in...  41.1 us

profile of v4, /device:TPU:8, one launch (start us, length us, event | category | flops | bytes accessed | tf_op | source)
XLA Modules:
  0.0 41.9 jit_solution(12880932332435765998)
XLA Ops:
  0.0 41.1 %shard_map.46 = f32[64,2048]{1,0:T(8,128)S(1)} custom-call(bf16[32,2048]{1,0:T(8,128)(2,1)} %signal.1, s32[8,32,1024]{2,1,0:T(8,128)} %delay.1, f32[32,1024]{1,0:T(8,128)} %fraction.1, f32[32,1024]{1,0:T(8,128)} %weight.1), custom_call_target="tpu_custom_call" | custom-call | tf_op jit(solution)/shard_map/pallas_call | solution.py:374
  41.1 0.8 %copy.6 = f32[64,2048]{1,0:T(8,128)} copy(f32[64,2048]{1,0:T(8,128)S(1)} %shard_map.46) | data formatting | bytes 1048576

commit v5 on v4

--- a/solution.py
+++ b/solution.py
@@ -177,11 +177,12 @@
     send_piece(1).start()
     loads[0].wait()
     loads[1].wait()
-    for k in range(2):
+    for k in (core, 1 - core):
         def put(half, i, v, k=k):
             fw[half, k, :, pl.ds(i * 128, 128)] = v
         halves(lambda i, k=k: fwraw[k, :, pl.ds(i * 128, 128)], put)
-    send_fw().start()
+        if k is core:
+            send_fw().start()
 
     def compact(b):
         def put(half, i, v):

time: 42 us -> 42 us (level)
  no operation moved by 1% of the time
where the time goes in v5:
time: 42 us; the launch traced here: 41.9 us
  Pallas kernels  41.1 us (98%)
  local copies, waits for them, and re-layouts  0.8 us (2%)
    pallas_call x1, Pallas kernels, shards(): pl.pallas_call(kernel, out_shape=pltpu.VMEM((FOCUS // 16, TIME), F32), in...  41.1 us

profile of v5, /device:TPU:8, one launch (start us, length us, event | category | flops | bytes accessed | tf_op | source)
XLA Modules:
  0.0 41.9 jit_solution(16735797321121719185)
XLA Ops:
  0.0 41.1 %shard_map.46 = f32[64,2048]{1,0:T(8,128)S(1)} custom-call(bf16[32,2048]{1,0:T(8,128)(2,1)} %signal.1, s32[8,32,1024]{2,1,0:T(8,128)} %delay.1, f32[32,1024]{1,0:T(8,128)} %fraction.1, f32[32,1024]{1,0:T(8,128)} %weight.1), custom_call_target="tpu_custom_call" | custom-call | tf_op jit(solution)/shard_map/pallas_call | solution.py:375
  41.1 0.8 %copy.6 = f32[64,2048]{1,0:T(8,128)} copy(f32[64,2048]{1,0:T(8,128)S(1)} %shard_map.46) | data formatting | bytes 1048576
